TPU v7x, 32 devices: a whole 2x2x4 slice. The times are simulated.
32 devices in a mesh: dp: 2 (over x), pipe: 4 (over z), tensor: 4 (over y, core).
Axes of the slice: x: 2, y: 2, z: 4, core: 2. Of those that a mesh axis runs over, the one named last changes fastest.
Arguments:
- inputs: bfloat16 [4, 3072, 8192], P('pipe', 'dp', 'tensor'), may hold values from -6 to 6
- upstream: bfloat16 [4, 3072, 8192], P('pipe', 'dp', 'tensor'), may hold values from -6 to 6
- factor_one: bfloat16 [4, 32, 4, 256, 256], P('pipe', 'tensor'), may hold values from -0.375 to 0.375
- factor_two: bfloat16 [4, 128, 256, 256], P('pipe', 'tensor'), may hold values from -0.375 to 0.375
- factor_three: bfloat16 [4, 128, 256, 256], P('pipe', 'tensor'), may hold values from -0.375 to 0.375
- factor_four: bfloat16 [4, 32, 4, 256, 256], P('pipe', 'tensor'), may hold values from -0.1875 to 0.1875
Outputs:
- y_next: bfloat16 [4, 3072, 8192], P('pipe', 'dp', 'tensor')
- dx_prev: bfloat16 [4, 3072, 8192], P('pipe', 'dp', 'tensor')
- grad_one: float32 [4, 32, 4, 256, 256], P('pipe', 'tensor')
- grad_two: float32 [4, 128, 256, 256], P('pipe', 'tensor')
- grad_three: float32 [4, 128, 256, 256], P('pipe', 'tensor')
- grad_four: float32 [4, 32, 4, 256, 256], P('pipe', 'tensor')
All inputs are finite; a program needn't handle non-finite values.
Results may differ from a plain program's by a relative error of at most 0.0068.
Values may be sent and summed in bfloat16 or wider, within the bound.
A program may use at most 384 MiB of HBM per device.

v0:
```python
import jax
import jax.numpy as jnp
from jax import lax
from jax.sharding import PartitionSpec as P


def shifted(value, axis, steps):
    count = lax.axis_size(axis)
    leading, last = (max(0, -steps), min(count, count - steps))
    return lax.ppermute(value, axis, [(source, source + steps) for source in range(leading, last)])


def to_peers(blocks, parts):
    rows, local, width = blocks.shape
    inner = width // (parts * local)
    shaped = blocks.reshape(rows, local, parts, local, inner)
    return shaped.transpose(0, 2, 1, 3, 4).reshape(rows, parts, local * local * inner)


def from_peers(received, local):
    rows, parts, flat = received.shape
    inner = flat // (local * local)
    shaped = received.reshape(rows, parts, local, local, inner)
    return shaped.transpose(0, 3, 1, 2, 4).reshape(rows, local, parts * local * inner)


def shards(inputs, upstream, factor_one, factor_two, factor_three, factor_four):
    parts = lax.axis_size("tensor")
    acts = inputs[0]
    grad_out = upstream[0]
    first = factor_one[0]
    second = factor_two[0]
    third = factor_three[0]
    fourth = factor_four[0]
    groups, expand, bsize = (first.shape[0], first.shape[1], first.shape[2])
    local = groups * expand
    rows = acts.shape[0]
    grouped = acts.reshape(rows, groups, bsize)
    lifted = (
        jnp.einsum("tgi,gkij->tgkj", grouped, first, preferred_element_type=jnp.float32)
        .astype(jnp.bfloat16)
        .reshape(rows, local, bsize)
    )
    outbound = to_peers(lifted, parts)
    mixed = from_peers(
        lax.all_to_all(outbound, "tensor", split_axis=1, concat_axis=1, tiled=True), local
    )
    preact = jnp.einsum("tcj,cjn->tcn", mixed, second, preferred_element_type=jnp.float32)
    active = jax.nn.gelu(preact).astype(jnp.bfloat16)
    mixed, preact, active = (mixed, preact, active)
    narrowed = jnp.einsum("tcn,cno->tco", active, third, preferred_element_type=jnp.float32).astype(
        jnp.bfloat16
    )
    outbound = to_peers(narrowed, parts)
    spread = from_peers(
        lax.all_to_all(outbound, "tensor", split_axis=1, concat_axis=1, tiled=True), local
    )
    count = spread.shape[0]
    output = jnp.einsum(
        "tgkr,gkro->tgo",
        spread.reshape(count, groups, expand, bsize),
        fourth,
        preferred_element_type=jnp.float32,
    ).astype(jnp.bfloat16)
    spread, output = (spread, output.reshape(count, groups * bsize))
    y_next = shifted(output[None], "pipe", 1)
    grad_grouped = grad_out.reshape(rows, groups, bsize)
    spread_four = spread.reshape(rows, groups, expand, bsize)
    grad_spread = (
        jnp.einsum("tgo,gkro->tgkr", grad_grouped, fourth, preferred_element_type=jnp.float32)
        .astype(jnp.bfloat16)
        .reshape(rows, local, bsize)
    )
    grad_four = jnp.einsum(
        "tgkr,tgo->gkro", spread_four, grad_grouped, preferred_element_type=jnp.float32
    )
    outbound = to_peers(grad_spread, parts)
    grad_narrow = from_peers(
        lax.all_to_all(outbound, "tensor", split_axis=1, concat_axis=1, tiled=True), local
    )
    grad_active = jnp.einsum("tco,cno->tcn", grad_narrow, third, preferred_element_type=jnp.float32)
    grad_narrow, grad_active = (grad_narrow, grad_active)
    grad_three = jnp.einsum("tcn,tco->cno", active, grad_narrow, preferred_element_type=jnp.float32)
    pulled = jax.vjp(jax.nn.gelu, preact)[1]
    grad_pre = pulled(grad_active)[0].astype(jnp.bfloat16)
    grad_two = jnp.einsum("tcj,tcn->cjn", mixed, grad_pre, preferred_element_type=jnp.float32)
    grad_mixed = jnp.einsum(
        "tcn,cjn->tcj", grad_pre, second, preferred_element_type=jnp.float32
    ).astype(jnp.bfloat16)
    outbound = to_peers(grad_mixed, parts)
    grad_lift = from_peers(
        lax.all_to_all(outbound, "tensor", split_axis=1, concat_axis=1, tiled=True), local
    )
    count = grad_lift.shape[0]
    grad_input = jnp.einsum(
        "tgkj,gkij->tgi",
        grad_lift.reshape(count, groups, expand, bsize),
        first,
        preferred_element_type=jnp.float32,
    ).astype(jnp.bfloat16)
    grad_lift, grad_input = (grad_lift, grad_input.reshape(count, groups * bsize))
    dx_prev = shifted(grad_input[None], "pipe", -1)
    grad_one = jnp.einsum(
        "tgi,tgkj->gkij",
        grouped,
        grad_lift.reshape(rows, groups, expand, bsize),
        preferred_element_type=jnp.float32,
    )
    grad_one, grad_two, grad_three, grad_four = lax.psum(
        (grad_one, grad_two, grad_three, grad_four), "dp"
    )
    return (y_next, dx_prev, grad_one[None], grad_two[None], grad_three[None], grad_four[None])


def solution(mesh):
    return jax.shard_map(
        shards,
        mesh=mesh,
        in_specs=(
            P("pipe", "dp", "tensor"),
            P("pipe", "dp", "tensor"),
            P("pipe", "tensor", None, None, None),
            P("pipe", "tensor", None, None),
            P("pipe", "tensor", None, None),
            P("pipe", "tensor", None, None, None),
        ),
        out_specs=(
            P("pipe", "dp", "tensor"),
            P("pipe", "dp", "tensor"),
            P("pipe", "tensor", None, None, None),
            P("pipe", "tensor", None, None),
            P("pipe", "tensor", None, None),
            P("pipe", "tensor", None, None, None),
        ),
        check_vma=False,
    )
```

profile of v0, /device:TPU:0, one launch (start us, length us, event | category | flops | bytes accessed | tf_op | source)
XLA Modules:
  0.0 2246.2 jit_solution(13473191419759393641)
XLA Ops:
  30.7 48.7 %reshape_reshape.14 = bf16[1536,32,4,32,2]{0,4,3,2,1:T(2,128)(2,1)} reshape(bf16[1536,8,4,256]{0,3,2,1:T(8,128)(2,1)} %convert_bitcast_fusion.3) | data formatting | bytes 50331648 | tf_op jit(solution)/shard_map/reshape;reshape | solution.py:16
  79.5 62.1 %copy.53 = bf16[1536,32,4,32,2]{0,2,4,3,1:T(4,128)(2,1)} copy(bf16[1536,32,4,32,2]{0,4,3,2,1:T(2,128)(2,1)} %reshape_reshape.14) | data formatting | bytes 50331648 | tf_op jit(solution)/shard_map/reshape;reshape | solution.py:16
  197.4 48.7 %reshape_reshape.16 = bf16[1536,32,4,32,2]{0,4,3,2,1:T(2,128)(2,1)} reshape(bf16[1536,8,4,256]{0,3,2,1:T(8,128)(2,1)} %convert_bitcast_fusion.1) | data formatting | bytes 50331648 | tf_op jit(solution)/shard_map/reshape;reshape | solution.py:16
  246.0 62.1 %copy.67 = bf16[1536,32,4,32,2]{0,2,4,3,1:T(4,128)(2,1)} copy(bf16[1536,32,4,32,2]{0,4,3,2,1:T(2,128)(2,1)} %reshape_reshape.16) | data formatting | bytes 50331648 | tf_op jit(solution)/shard_map/reshape;reshape | solution.py:16
  332.3 115.6 %all-to-all-done = bf16[1536,4,2048]{0,2,1:T(8,128)(2,1)} async-done(((bf16[1536,4,2048]{0,2,1:T(8,128)(2,1)}), bf16[1536,4,2048]{0,2,1:T(8,128)(2,1)}, u32[]{:S(2)}, u32[]{:S(2)}) %all-to-all-start) | async-done | bytes 25165856 | tf_op jit(solution)/shard_map/all_to_all | solution.py:46
  456.7 32.3 %copy.55 = bf16[1536,4,2048]{0,1,2:T(4,128)(2,1)} copy(bf16[1536,4,2048]{0,2,1:T(8,128)(2,1)} %all-to-all-done) | data formatting | bytes 50331648 | tf_op jit(solution)/shard_map/all_to_all | solution.py:46
  513.7 34.2 %fusion.11 = f32[32,1536,256]{2,1,0:T(8,128)} fusion(bf16[1536,32,256]{0,1,2:T(8,128)(2,1)} %bitcast.144, bf16[1,32,256,256]{3,2,1,0:T(8,128)(2,1)} %param.9), kind=kOutput, calls=%fused_computation.20 | convolution fusion | flops 6442450944 | bytes 79691776 | tf_op jit(solution)/shard_map/tcj,cjn->tcn/dot_general | solution.py:48
  547.9 32.7 %convert_bitcast_fusion.2 = bf16[1536,32,256]{0,2,1:T(8,128)(2,1)} fusion(bf16[1,32,256,256]{3,2,1,0:T(8,128)(2,1)} %param.10, f32[32,1536,256]{2,1,0:T(8,128)} %fusion.11), kind=kOutput, calls=%fused_computation.18 | convolution fusion | flops 6568280064 | bytes 79691776 | tf_op jit(solution)/shard_map/tcn,cno->tco/dot_general | solution.py:51
  580.6 48.7 %reshape.51 = bf16[1536,32,4,32,2]{0,4,3,2,1:T(2,128)(2,1)} reshape(bf16[1536,32,256]{0,2,1:T(8,128)(2,1)} %convert_bitcast_fusion.2) | data formatting | bytes 50331648 | tf_op jit(solution)/shard_map/reshape | solution.py:16
  629.3 62.1 %copy.59 = bf16[1536,32,4,32,2]{0,2,4,3,1:T(4,128)(2,1)} copy(bf16[1536,32,4,32,2]{0,4,3,2,1:T(2,128)(2,1)} %reshape.51) | data formatting | bytes 50331648 | tf_op jit(solution)/shard_map/reshape | solution.py:16
  738.4 32.3 %copy.69 = bf16[1536,4,2048]{0,1,2:T(4,128)(2,1)} copy(bf16[1536,4,2048]{0,2,1:T(8,128)(2,1)} %all-to-all-done.2) | data formatting | bytes 50331648 | tf_op jit(solution)/shard_map/all_to_all | solution.py:79
  826.9 43.8 %fusion.6 = bf16[1536,32,256]{2,0,1:T(8,128)(2,1)} fusion(f32[32,1536,256]{2,1,0:T(8,128)} %fusion.11, bf16[1536,32,256]{2,0,1:T(8,128)(2,1)} %copy.71, bf16[1,32,256,256]{3,2,1,0:T(8,128)(2,1)} %param.10), kind=kOutput, calls=%fused_computation.8 | convolution fusion | flops 6694109184 | bytes 104857600 | tf_op jit(solution)/shard_map/tco,cno->tcn/dot_general | solution.py:81
  891.6 49.1 %reshape.57 = bf16[1536,32,4,32,2]{0,4,3,2,1:T(2,128)(2,1)} reshape(bf16[1536,32,256]{0,2,1:T(8,128)(2,1)} %convert_bitcast_fusion) | data formatting | bytes 50331648 | tf_op jit(solution)/shard_map/reshape | solution.py:16
  940.7 62.1 %copy.72 = bf16[1536,32,4,32,2]{0,2,4,3,1:T(4,128)(2,1)} copy(bf16[1536,32,4,32,2]{0,4,3,2,1:T(2,128)(2,1)} %reshape.57) | data formatting | bytes 50331648 | tf_op jit(solution)/shard_map/reshape | solution.py:16
  1097.2 32.3 %copy.61 = bf16[1536,4,2048]{0,1,2:T(4,128)(2,1)} copy(bf16[1536,4,2048]{0,2,1:T(8,128)(2,1)} %all-to-all-done.1) | data formatting | bytes 50331648 | tf_op jit(solution)/shard_map/all_to_all | solution.py:56
  1129.5 36.0 %copy.62 = bf16[1536,32,4,32,2]{0,4,3,2,1:T(2,128)(2,1)} copy(bf16[1536,32,4,32,2]{0,2,4,1,3:T(4,128)(2,1)} %bitcast.153) | data formatting | bytes 50331648 | tf_op jit(solution)/shard_map/transpose | solution.py:24
  1165.5 50.5 %reshape_reshape.15 = bf16[1536,8,4,256]{0,3,2,1:T(8,128)(2,1)} reshape(bf16[1536,32,4,32,2]{0,4,3,2,1:T(2,128)(2,1)} %copy.62) | data formatting | bytes 50331648 | tf_op jit(solution)/shard_map/reshape;reshape | solution.py:61
  1216.0 92.3 %all-to-all-done.3 = bf16[1536,4,2048]{0,2,1:T(8,128)(2,1)} async-done(((bf16[1536,4,2048]{0,2,1:T(8,128)(2,1)}), bf16[1536,4,2048]{0,2,1:T(8,128)(2,1)}, u32[]{:S(2)}, u32[]{:S(2)}) %all-to-all-start.3) | async-done | bytes 25165856 | tf_op jit(solution)/shard_map/all_to_all | solution.py:92
  1308.3 32.3 %copy.74 = bf16[1536,4,2048]{0,1,2:T(4,128)(2,1)} copy(bf16[1536,4,2048]{0,2,1:T(8,128)(2,1)} %all-to-all-done.3) | data formatting | bytes 50331648 | tf_op jit(solution)/shard_map/all_to_all | solution.py:92
  1340.6 36.0 %copy.75 = bf16[1536,32,4,32,2]{0,4,3,2,1:T(2,128)(2,1)} copy(bf16[1536,32,4,32,2]{0,2,4,1,3:T(4,128)(2,1)} %bitcast.154) | data formatting | bytes 50331648 | tf_op jit(solution)/shard_map/transpose | solution.py:24
  1376.6 50.7 %reshape_reshape.17 = bf16[1536,8,4,256]{0,3,2,1:T(8,128)(2,1)} reshape(bf16[1536,32,4,32,2]{0,4,3,2,1:T(2,128)(2,1)} %copy.75) | data formatting | bytes 50331648 | tf_op jit(solution)/shard_map/reshape;reshape | solution.py:97
  1516.7 105.0 %collective-permute-done = bf16[1,1536,2048]{2,1,0:T(8,128)(2,1)} collective-permute-done((bf16[1,1536,2048]{2,1,0:T(8,128)(2,1)}, bf16[1,1536,2048]{2,1,0:T(8,128)(2,1)}, u32[]{:S(2)}, u32[]{:S(2)}) %collective-permute-start) | collective-permute-done | bytes 6291488 | tf_op jit(solution)/shard_map/ppermute | solution.py:10
  1621.7 33.3 %collective-permute-done.1 = bf16[1,1536,2048]{2,1,0:T(8,128)(2,1)} collective-permute-done((bf16[1,1536,2048]{2,1,0:T(8,128)(2,1)}, bf16[1,1536,2048]{2,1,0:T(8,128)(2,1)}, u32[]{:S(2)}, u32[]{:S(2)}) %collective-permute-start.1) | collective-permute-done | bytes 6291488 | tf_op jit(solution)/shard_map/ppermute | solution.py:10
  1655.0 546.6 %all-reduce.3.cloned.1.call-done = (f32[1,8,4,256,256]{3,4,2,1,0:T(8,128)}, f32[1,32,256,256]{3,2,1,0:T(8,128)}, f32[1,32,256,256]{3,2,1,0:T(8,128)}, f32[1,8,4,256,256]{4,3,2,1,0:T(8,128)}) async-done(((f32[1,8,4,256,256]{3,4,2,1,0:T(8,128)}, f32[1,32,256,256]{3,2,1,0:T(8,128)}, f32[1,32,256,256]{3,2,1,0:T(8,128)}, f32[1,8,4,256,256]{4,3,2,1,0:T(8,128)}), (f32[1,8,4,256,256]{3,4,2,1,0:T(8,128)}, ...) | async-done | bytes 33554448 | tf_op jit(solution)/shard_map/psum | solution.py:109
  (46 shorter events, 482.2 us)
Async XLA Ops:
  165.6 282.2 %all-to-all-start = ((bf16[1536,4,2048]{0,2,1:T(8,128)(2,1)}), bf16[1536,4,2048]{0,2,1:T(8,128)(2,1)}, u32[]{:S(2)}, u32[]{:S(2)}) async-start(bf16[1536,4,2048]{0,2,1:T(8,128)(2,1)} %copy.54), calls=%async_computation | async-start | bytes 50331648 | tf_op jit(solution)/shard_map/all_to_all | solution.py:46
  447.8 281.8 %all-to-all-start.2 = ((bf16[1536,4,2048]{0,2,1:T(8,128)(2,1)}), bf16[1536,4,2048]{0,2,1:T(8,128)(2,1)}, u32[]{:S(2)}, u32[]{:S(2)}) async-start(bf16[1536,4,2048]{0,2,1:T(8,128)(2,1)} %copy.68), calls=%async_computation.2 | async-start | bytes 50331648 | tf_op jit(solution)/shard_map/all_to_all | solution.py:79
  729.7 297.2 %all-to-all-start.1 = ((bf16[1536,4,2048]{0,2,1:T(8,128)(2,1)}), bf16[1536,4,2048]{0,2,1:T(8,128)(2,1)}, u32[]{:S(2)}, u32[]{:S(2)}) async-start(bf16[1536,4,2048]{0,2,1:T(8,128)(2,1)} %copy.60), calls=%async_computation.1 | async-start | bytes 50331648 | tf_op jit(solution)/shard_map/all_to_all | solution.py:56
  1026.9 281.4 %all-to-all-start.3 = ((bf16[1536,4,2048]{0,2,1:T(8,128)(2,1)}), bf16[1536,4,2048]{0,2,1:T(8,128)(2,1)}, u32[]{:S(2)}, u32[]{:S(2)}) async-start(bf16[1536,4,2048]{0,2,1:T(8,128)(2,1)} %copy.73), calls=%async_computation.3 | async-start | bytes 50331648 | tf_op jit(solution)/shard_map/all_to_all | solution.py:92
  1035.3 1166.4 %all-reduce.3.cloned.1.call-start = ((), (), s32[]{:S(2)}) async-start(), calls=%async_computation.4 | async-start | bytes 67108864 | tf_op jit(solution)/shard_map/psum | solution.py:109
  1482.6 139.1 %collective-permute-start = (bf16[1,1536,2048]{2,1,0:T(8,128)(2,1)}, bf16[1,1536,2048]{2,1,0:T(8,128)(2,1)}, u32[]{:S(2)}, u32[]{:S(2)}) collective-permute-start(bf16[1,1536,2048]{2,1,0:T(8,128)(2,1)} %copy.65), channel_id=1, source_target_pairs={{0,4},{4,8},{8,12},{1,5},{5,9},{9,13},{2,6},{6,10},{10,14},{3,7},{... | collective-permute-start | bytes 18874376 | tf_op jit(solution)/shard_map/ppermute | solution.py:10
  1515.4 139.6 %collective-permute-start.1 = (bf16[1,1536,2048]{2,1,0:T(8,128)(2,1)}, bf16[1,1536,2048]{2,1,0:T(8,128)(2,1)}, u32[]{:S(2)}, u32[]{:S(2)}) collective-permute-start(bf16[1,1536,2048]{2,1,0:T(8,128)(2,1)} %copy.77), channel_id=1, source_target_pairs={{4,0},{8,4},{12,8},{5,1},{9,5},{13,9},{6,2},{10,6},{14,10},{7,3},{... | collective-permute-start | bytes 18874376 | tf_op jit(solution)/shard_map/ppermute | solution.py:10
  2210.8 21.3 slice-start.2
  2217.5 14.6 slice-start.3
  2217.5 18.0 slice-start
  2224.3 11.2 slice-start.1
Sparse Core Ops, SparseCore 0:
  1458.2 743.3 all-reduce.2
where the time goes:
time: 2260 us; the launch traced here: 2250 us
  local copies, waits for them, and re-layouts  994 us (44%)
  waiting for transfers between devices  907 us (40%)
  matrix products  288 us (13%)
  starting transfers between devices  42.2 us (2%)
    psum x1, waiting for transfers between devices, shards(): lax.psum((grad_one, grad_two, grad_three, grad_four), 'dp')  547 us
    all_to_all x4, waiting for transfers between devices, shards(): lax.all_to_all(outbound, 'tensor', split_axis=1, concat_axis=1, tiled=True)  222 us
    reshape x4, local copies, waits for them, and re-layouts, to_peers(): shaped = blocks.reshape(rows, local, parts, local, inner)  222 us
    another operation x4, local copies, waits for them, and re-layouts, to_peers(): shaped = blocks.reshape(rows, local, parts, local, inner)  222 us
    ppermute x2, waiting for transfers between devices, shifted(): lax.ppermute(value, axis, [(source, source + steps) for source in range(l...  138 us
    all_to_all x4, local copies, waits for them, and re-layouts, shards(): lax.all_to_all(outbound, 'tensor', split_axis=1, concat_axis=1, tiled=True)  129 us
    transpose x4, local copies, waits for them, and re-layouts, from_peers(): shaped.transpose(0, 3, 1, 2, 4).reshape(rows, local, parts * local * inner)  121 us
    reshape x4, local copies, waits for them, and re-layouts, to_peers(): shaped.transpose(0, 2, 1, 3, 4).reshape(rows, parts, local * local * inner)  96.4 us
  transfers between devices with their start and end apart: 7, of which 6 were waited for; matrix products, arithmetic and copies ran while one was open for 42% of the time, Pallas kernels for 0%

commit v1 on v0

v1 whole, which is shorter than its diff:
```python
import functools
import math

import jax
import jax.numpy as jnp
from jax import lax
from jax.experimental import pallas as pl
from jax.experimental.pallas import tpu as pltpu
from jax.sharding import PartitionSpec as P

F32, BF16 = jnp.float32, jnp.bfloat16
HALVES = 2
ROOT = math.sqrt(2.0 / math.pi)
CUBE = 0.044715
VMEM = 48 * 2**20


def params():
    return pltpu.CompilerParams(vmem_limit_bytes=VMEM)


def contract(a, b, da, db):
    return lax.dot_general(a, b, (((da,), (db,)), ((), ())), preferred_element_type=F32)


def exchange(value, axis, mask):
    count = lax.axis_size(axis)
    return lax.ppermute(value, axis, [(i, i ^ mask) for i in range(count)])


def shifted(value, axis, steps):
    count = lax.axis_size(axis)
    leading, last = (max(0, -steps), min(count, count - steps))
    return lax.ppermute(value, axis, [(source, source + steps) for source in range(leading, last)])


def lift_kernel(spot, x_ref, w_ref, *refs):
    out_ref = refs[-1]
    local = out_ref.shape[0]
    bsize = w_ref.shape[2]
    parts = []
    for j in range(2):
        block = contract(w_ref[j], x_ref[:, j * bsize:(j + 1) * bsize], 1, 1)
        parts.append(block.reshape(local, block.shape[0] // local, block.shape[1]))
    out_ref[...] = jnp.concatenate(parts, axis=1).astype(BF16)


def lift(spot, x, w, buffer, local, width):
    groups, rows, bsize = w.shape
    tokens = x.shape[0]
    pairs = groups // 2
    in_specs = [
        pl.BlockSpec((tokens, 2 * bsize), lambda i, s: (0, i)),
        pl.BlockSpec((2, rows, bsize), lambda i, s: (i, 0, 0)),
    ]
    args = [x, w]
    aliases = {}
    if buffer is not None:
        in_specs.append(pl.BlockSpec(memory_space=pl.ANY))
        args.append(buffer)
        aliases = {3: 0}
    high = 2 * rows // local
    return pl.pallas_call(
        lift_kernel,
        grid_spec=pltpu.PrefetchScalarGridSpec(
            num_scalar_prefetch=1,
            grid=(pairs,),
            in_specs=in_specs,
            out_specs=pl.BlockSpec((local, high, tokens), lambda i, s: (0, s[0] * pairs + i, 0)),
        ),
        out_shape=jax.ShapeDtypeStruct((local, width, tokens), BF16),
        input_output_aliases=aliases,
        compiler_params=params(),
        cost_estimate=pl.CostEstimate(
            flops=2 * groups * rows * bsize * tokens,
            bytes_accessed=2 * (groups * bsize * tokens + w.size + groups * rows * tokens),
            transcendentals=0,
        ),
        name="lift",
    )(spot, *args)


def middle_kernel(adds, mixed_ref, gn_ref, two_ref, three_ref, *refs):
    if adds:
        old_two, old_three, narrow_ref, gm_ref, g2_ref, g3_ref = refs
    else:
        narrow_ref, gm_ref, g2_ref, g3_ref = refs
    mixed, gn, two, three = mixed_ref[0], gn_ref[0], two_ref[0], three_ref[0]
    pre = contract(two, mixed, 0, 0)
    grad_active = contract(three, gn, 1, 0)
    square = pre * pre
    tanh = jnp.tanh(pre * (ROOT + (ROOT * CUBE) * square))
    half = 0.5 + 0.5 * tanh
    active = (pre * half).astype(BF16)
    slope = half + (0.5 * pre) * (1.0 - tanh * tanh) * (ROOT + (3.0 * ROOT * CUBE) * square)
    grad_pre = (grad_active * slope).astype(BF16)
    narrow_ref[0] = contract(three, active, 0, 0).astype(BF16)
    gm_ref[0] = contract(two, grad_pre, 1, 0).astype(BF16)
    g3 = contract(active, gn, 1, 1)
    g2 = contract(mixed, grad_pre, 1, 1)
    if adds:
        g3 = g3 + old_three[0]
        g2 = g2 + old_two[0]
    g2_ref[0] = g2
    g3_ref[0] = g3


def middle(mixed, gn, two, three, olds):
    local, width, tokens = mixed.shape
    data = pl.BlockSpec((1, width, tokens), lambda c: (c, 0, 0))
    factor = pl.BlockSpec((1, width, width), lambda c: (c, 0, 0))
    grads = jax.ShapeDtypeStruct((local, width, width), F32)
    hidden = jax.ShapeDtypeStruct(mixed.shape, BF16)
    return pl.pallas_call(
        functools.partial(middle_kernel, bool(olds)),
        grid=(local,),
        in_specs=[data, data, factor, factor] + [factor] * len(olds),
        out_specs=[data, data, factor, factor],
        out_shape=[hidden, hidden, grads, grads],
        compiler_params=params(),
        cost_estimate=pl.CostEstimate(
            flops=12 * local * width * width * tokens,
            bytes_accessed=8 * local * width * tokens + 12 * local * width * width,
            transcendentals=local * width * tokens,
        ),
        name="middle",
    )(mixed, gn, two, three, *olds)


def last_kernel(adds, olds, spot, narrow_ref, gm_ref, one_ref, four_ref, x_ref, up_ref, *refs):
    refs = list(refs)
    added = [refs.pop(0) for _ in range(2)] if adds else None
    kept = [refs.pop(0) for _ in range(2)] if olds else None
    out_ref, gi_ref, g1_ref, g4_ref = refs
    bsize = one_ref.shape[2]
    rows = one_ref.shape[1]
    local, high, tokens = narrow_ref.shape
    low = high // 2
    narrow = narrow_ref[...].astype(F32)
    lifted = gm_ref[...].astype(F32)
    for j in range(2):
        cols = slice(j * bsize, (j + 1) * bsize)
        spread = narrow[:, j * low:(j + 1) * low].reshape(rows, tokens).astype(BF16)
        grad_lift = lifted[:, j * low:(j + 1) * low].reshape(rows, tokens).astype(BF16)
        out = contract(spread, four_ref[j], 0, 0)
        gi = contract(grad_lift, one_ref[j], 0, 0)
        if adds:
            out = out + added[0][:, cols].astype(F32)
            gi = gi + added[1][:, cols].astype(F32)
        out_ref[:, cols] = out.astype(BF16)
        gi_ref[:, cols] = gi.astype(BF16)
        g1 = contract(grad_lift, x_ref[:, cols], 1, 0)
        g4 = contract(spread, up_ref[:, cols], 1, 0)
        if olds:
            g1 = g1 + kept[0][j]
            g4 = g4 + kept[1][j]
        g1_ref[j] = g1
        g4_ref[j] = g4


def last(spot, narrow, gm, one, four, x, up, added, olds):
    local, width, tokens = narrow.shape
    groups, rows, bsize = one.shape
    pairs = groups // 2
    high = 2 * rows // local
    hidden = pl.BlockSpec((local, high, tokens), lambda i, s: (0, s[0] * pairs + i, 0))
    factor = pl.BlockSpec((2, rows, bsize), lambda i, s: (i, 0, 0))
    data = pl.BlockSpec((tokens, 2 * bsize), lambda i, s: (0, i))
    return pl.pallas_call(
        functools.partial(last_kernel, bool(added), bool(olds)),
        grid_spec=pltpu.PrefetchScalarGridSpec(
            num_scalar_prefetch=1,
            grid=(pairs,),
            in_specs=[hidden, hidden, factor, factor, data, data]
            + [data] * len(added) + [factor] * len(olds),
            out_specs=[data, data, factor, factor],
        ),
        out_shape=[
            jax.ShapeDtypeStruct(x.shape, BF16),
            jax.ShapeDtypeStruct(x.shape, BF16),
            jax.ShapeDtypeStruct(one.shape, F32),
            jax.ShapeDtypeStruct(one.shape, F32),
        ],
        compiler_params=params(),
        cost_estimate=pl.CostEstimate(
            flops=8 * groups * rows * bsize * tokens,
            bytes_accessed=4 * groups * rows * tokens + 8 * x.size + 12 * one.size,
            transcendentals=0,
        ),
        name="last",
    )(spot, narrow, gm, one, four, x, up, *added, *olds)


def gather(value, bits):
    held = {0: value}
    for bit in reversed(bits):
        for q in list(held):
            held[q ^ bit] = exchange(held[q], "tensor", bit)
    return held


def shards(inputs, upstream, factor_one, factor_two, factor_three, factor_four):
    parts = lax.axis_size("tensor")
    bits = [1 << b for b in range(parts.bit_length() - 1)]
    me = lax.axis_index("tensor")
    acts, grad_out = inputs[0], upstream[0]
    first, second, third, fourth = factor_one[0], factor_two[0], factor_three[0], factor_four[0]
    groups, expand, bsize = first.shape[:3]
    local = second.shape[0]
    inner = bsize // (parts * local)
    rows = local * expand * inner
    tokens = acts.shape[0] // HALVES
    spots = {q: (me ^ q).astype(jnp.int32).reshape(1) for q in range(parts)}

    ones = first.reshape(groups, expand, bsize, parts, local, inner).transpose(3, 0, 4, 1, 5, 2)
    ones = ones.reshape(parts, groups, rows, bsize)
    fours = fourth.reshape(groups, expand, parts, local, inner, bsize).transpose(2, 0, 3, 1, 4, 5)
    fours = fours.reshape(parts, groups, rows, bsize)
    one, four = {}, {}
    for q in reversed(range(parts)):
        pair = jnp.stack([
            lax.dynamic_index_in_dim(ones, me ^ q, 0, False),
            lax.dynamic_index_in_dim(fours, me ^ q, 0, False),
        ])
        if q:
            pair = exchange(pair, "tensor", q)
        one[q], four[q] = pair[0], pair[1]

    grads_mid, grads_end = (), {q: () for q in range(parts)}
    y_parts, dx_parts = [], []
    gathered = []
    for h in range(HALVES):
        rows_h = slice(h * tokens, (h + 1) * tokens)
        gathered.append((gather(acts[rows_h], bits), gather(grad_out[rows_h], bits)))
    for h in range(HALVES):
        xs, ups = gathered[h]
        mixed = grad_narrow = None
        for q in xs:
            mixed = lift(spots[q], xs[q], one[q], mixed, local, bsize)
            grad_narrow = lift(spots[q], ups[q], four[q], grad_narrow, local, bsize)
        narrow, grad_mixed, g2, g3 = middle(mixed, grad_narrow, second, third, grads_mid)
        grads_mid = (g2, g3)
        totals = {}
        for q in sorted(range(parts), key=lambda q: (-(q & -2), -(q & 1))):
            added = ()
            if not q & 1:
                added = tuple(exchange(t, "tensor", 1) for t in totals.pop(q ^ 1))
            out, gi, g1, g4 = last(
                spots[q], narrow, grad_mixed, one[q], four[q], xs[q], ups[q], added, grads_end[q]
            )
            grads_end[q] = (g1, g4)
            totals[q] = (out, gi)
        for bit in bits[1:]:
            for q in [q for q in totals if q & bit]:
                came = [exchange(t, "tensor", bit) for t in totals.pop(q)]
                totals[q ^ bit] = tuple(
                    (t.astype(F32) + c.astype(F32)).astype(BF16)
                    for t, c in zip(totals[q ^ bit], came)
                )
        out, gi = totals[0]
        y_parts.append(shifted(out, "pipe", 1))
        dx_parts.append(shifted(gi, "pipe", -1))
    y_next = jnp.concatenate(y_parts, axis=0)[None]
    dx_prev = jnp.concatenate(dx_parts, axis=0)[None]

    mids = []
    for grad in grads_mid:
        mine = grad.astype(BF16)
        other = exchange(mine, "dp", 1)
        mids.append((mine.astype(F32) + other.astype(F32))[None])

    split = lax.axis_index("dp")
    cut = groups // 2
    own = []
    for q in range(parts):
        both = jnp.stack(grads_end[q])
        keep = lax.dynamic_slice_in_dim(both, split * cut, cut, 1)
        give = lax.dynamic_slice_in_dim(both, (1 - split) * cut, cut, 1).astype(BF16)
        total = (keep + exchange(give, "dp", 1).astype(F32)).astype(BF16)
        own.append(exchange(total, "tensor", q) if q else total)
    stacked = jnp.stack(own)
    other = exchange(stacked, "dp", 1)
    low = jnp.where(split == 0, stacked, other)
    high = jnp.where(split == 0, other, stacked)
    whole = jnp.concatenate([low, high], axis=2)
    whole = jnp.stack([lax.dynamic_index_in_dim(whole, me ^ p, 0, False) for p in range(parts)])
    whole = whole.reshape(parts, 2, groups, local, expand, inner, bsize)
    grad_one = whole[:, 0].transpose(1, 3, 5, 0, 2, 4).reshape(first.shape).astype(F32)
    grad_four = whole[:, 1].transpose(1, 3, 0, 2, 4, 5).reshape(fourth.shape).astype(F32)
    return (y_next, dx_prev, grad_one[None], mids[0], mids[1], grad_four[None])


def solution(mesh):
    specs = (
        P("pipe", "dp", "tensor"),
        P("pipe", "dp", "tensor"),
        P("pipe", "tensor", None, None, None),
        P("pipe", "tensor", None, None),
        P("pipe", "tensor", None, None),
        P("pipe", "tensor", None, None, None),
    )
    return jax.shard_map(shards, mesh=mesh, in_specs=specs, out_specs=specs, check_vma=False)
```

time: 2260 us -> 1250 us (0.55)
  local copies, waits for them, and re-layouts: 994 us -> 118 us
  matrix products: 288 us -> 0 us
  Pallas kernels: 0 us -> 246 us
  waiting for transfers between devices: 907 us -> 727 us
  other arithmetic: 0.01 us -> 103 us
    ppermute x0 -> x37, waiting for transfers between devices: none -> 727 us  [exchange(): return lax.ppermute(value, axis, [(i, i ^ mask) for i in range(count)])]
    psum x1 -> x0, waiting for transfers between devices: 547 us -> none  [shards(): lax.psum((grad_one, grad_two, grad_three, grad_four), 'dp')]
    another operation x8 -> x2, local copies, waits for them, and re-layouts: 340 us -> 14.9 us  [shards(): fourth.reshape(groups, expand, parts, local, inner, bsize)]
    reshape x9 -> x3, local copies, waits for them, and re-layouts: 350 us -> 27.4 us  [the longest x1 13.1 us: shards(): whole = whole.reshape(parts, 2, groups, local, expand, inner, bsize)]
    dot_general x12 -> x0, matrix products: 288 us -> none  [the longest x1 43.8 us: shards(): jnp.einsum('tco,cno->tcn', grad_narrow, third, preferred_element_type=jnp...]
    pallas_call x0 -> x26, Pallas kernels: none -> 246 us  [the longest x2 89.2 us: middle(): pl.pallas_call(functools.partial(middle_kernel, bool(olds)), grid=(local,...]
    all_to_all x4 -> x0, waiting for transfers between devices: 222 us -> none  [shards(): lax.all_to_all(outbound, 'tensor', split_axis=1, concat_axis=1, tiled=True)]
    ppermute x2 -> x4, waiting for transfers between devices: 138 us -> 0.01 us  [shifted(): lax.ppermute(value, axis, [(source, source + steps) for source in range(l...]
  transfers between devices with their start and end apart: 7 -> 41, of which waited for: 6 -> 14; matrix products, arithmetic and copies ran while one was open for 42% -> 12% of each run, Pallas kernels for 0% -> 20%
where the time goes in v1:
time: 1250 us; the launch traced here: 1240 us
  waiting for transfers between devices  727 us (58%)
  Pallas kernels  246 us (20%)
  local copies, waits for them, and re-layouts  118 us (9%)
  other arithmetic  103 us (8%)
  starting transfers between devices  41.6 us (3%)
    ppermute x37, waiting for transfers between devices, exchange(): return lax.ppermute(value, axis, [(i, i ^ mask) for i in range(count)])  727 us
    pallas_call x2, Pallas kernels, middle(): pl.pallas_call(functools.partial(middle_kernel, bool(olds)), grid=(local,...  89.2 us
    pallas_call x8, Pallas kernels, last(): pl.pallas_call(functools.partial(last_kernel, bool(added), bool(olds)), g...  84.4 us
    pallas_call x16, Pallas kernels, lift(): pl.pallas_call(lift_kernel, grid_spec=pltpu.PrefetchScalarGridSpec(num_sc...  72.8 us
    unnamed x92, local copies, waits for them, and re-layouts  34.4 us
    ppermute x37, starting transfers between devices, exchange(): return lax.ppermute(value, axis, [(i, i ^ mask) for i in range(count)])  28.5 us
  transfers between devices with their start and end apart: 41, of which 14 were waited for; matrix products, arithmetic and copies ran while one was open for 12% of the time, Pallas kernels for 20%

profile of v1, /device:TPU:0, one launch (start us, length us, event | category | flops | bytes accessed | tf_op | source)
XLA Modules:
  0.0 1238.3 jit_solution(43974227178718113)
XLA Ops:
  65.0 37.8 %collective-permute-done.5 = bf16[2,8,256,256]{3,2,1,0:T(8,128)(2,1)S(1)} collective-permute-done((bf16[2,8,256,256]{3,2,1,0:T(8,128)(2,1)}, bf16[2,8,256,256]{3,2,1,0:T(8,128)(2,1)S(1)}, u32[]{:S(2)}, u32[]{:S(2)}) %collective-permute-start.5) | collective-permute-done | bytes 2097184 | tf_op jit(solution)/shard_map/ppermute | solution.py:28
  106.6 40.8 %collective-permute-done.2 = bf16[2,8,256,256]{3,2,1,0:T(8,128)(2,1)} collective-permute-done((bf16[2,8,256,256]{3,2,1,0:T(8,128)(2,1)}, bf16[2,8,256,256]{3,2,1,0:T(8,128)(2,1)}, u32[]{:S(2)}, u32[]{:S(2)}) %collective-permute-start.2) | collective-permute-done | bytes 2097184 | tf_op jit(solution)/shard_map/ppermute | solution.py:28
  147.6 67.6 %collective-permute-done.6.x_ref.up_ref = bf16[768,2048]{1,0:T(8,128)(2,1)} collective-permute-done((bf16[768,2048]{1,0:T(8,128)(2,1)S(1)}, bf16[768,2048]{1,0:T(8,128)(2,1)}, u32[]{:S(2)}, u32[]{:S(2)}) %collective-permute-start.6) | collective-permute-done | bytes 3145760 | tf_op jit(solution)/shard_map/ppermute | solution.py:28
  219.0 63.7 %collective-permute-done.x_ref = bf16[768,2048]{1,0:T(8,128)(2,1)} collective-permute-done((bf16[768,2048]{1,0:T(8,128)(2,1)S(1)}, bf16[768,2048]{1,0:T(8,128)(2,1)}, u32[]{:S(2)}, u32[]{:S(2)}) %collective-permute-start) | collective-permute-done | bytes 3145760 | tf_op jit(solution)/shard_map/ppermute | solution.py:28
  284.9 65.2 %collective-permute-done.18.x_ref.up_ref = bf16[768,2048]{1,0:T(8,128)(2,1)} collective-permute-done((bf16[768,2048]{1,0:T(8,128)(2,1)S(1)}, bf16[768,2048]{1,0:T(8,128)(2,1)}, u32[]{:S(2)}, u32[]{:S(2)}) %collective-permute-start.18) | collective-permute-done | bytes 3145760 | tf_op jit(solution)/shard_map/ppermute | solution.py:28
  378.8 37.9 %collective-permute-done.15.x_ref = bf16[768,2048]{1,0:T(8,128)(2,1)} collective-permute-done((bf16[768,2048]{1,0:T(8,128)(2,1)}, bf16[768,2048]{1,0:T(8,128)(2,1)}, u32[]{:S(2)}, u32[]{:S(2)}) %collective-permute-start.15) | collective-permute-done | bytes 3145760 | tf_op jit(solution)/shard_map/ppermute | solution.py:28
  458.9 43.1 %middle.2 = (bf16[32,256,768]{2,1,0:T(8,128)(2,1)}, bf16[32,256,768]{2,1,0:T(8,128)(2,1)}, f32[32,256,256]{2,1,0:T(8,128)}, f32[32,256,256]{2,1,0:T(8,128)}) custom-call(bf16[32,256,768]{2,1,0:T(8,128)(2,1)} %lift.19.mixed_ref, bf16[32,256,768]{2,1,0:T(8,128)(2,1)} %lift.23.gn_ref, bf16[32,256,256]{2,1,0:T(8,128)(2,1)S(1)} %bitcast.84, ...), custom_call_target="tpu_custom_call" | custom-call | flops 19327352832 | bytes 75497472 | tf_op jit(solution)/shard_map/middle/pallas_call | solution.py:114
  534.6 46.1 %middle.3 = (bf16[32,256,768]{2,1,0:T(8,128)(2,1)}, bf16[32,256,768]{2,1,0:T(8,128)(2,1)}, f32[32,256,256]{2,1,0:T(8,128)}, f32[32,256,256]{2,1,0:T(8,128)}) custom-call(bf16[32,256,768]{2,1,0:T(8,128)(2,1)} %lift.27.mixed_ref, bf16[32,256,768]{2,1,0:T(8,128)(2,1)} %lift.31.gn_ref, bf16[32,256,256]{2,1,0:T(8,128)(2,1)S(1)} %bitcast.85, ...), custom_call_target="tpu_custom_call" | custom-call | flops 19327352832 | bytes 75497472 | tf_op jit(solution)/shard_map/middle/pallas_call | solution.py:114
  580.6 10.4 last.12
  594.9 10.2 last.14
  607.0 12.2 collective-permute-done.32
  619.2 21.5 %collective-permute-done.36 = bf16[2,4,256,256]{3,2,1,0:T(8,128)(2,1)S(1)} collective-permute-done((bf16[2,4,256,256]{3,2,1,0:T(8,128)(2,1)S(1)}, bf16[2,4,256,256]{3,2,1,0:T(8,128)(2,1)S(1)}, u32[]{:S(2)}, u32[]{:S(2)}) %collective-permute-start.36) | collective-permute-done | bytes 1048608 | tf_op jit(solution)/shard_map/ppermute | solution.py:28
  657.6 10.8 last.11
  669.8 11.8 last.15
  686.6 10.8 last.9
  698.8 11.7 last.13
  712.7 142.2 %collective-permute-done.34 = bf16[2,4,256,256]{3,2,1,0:T(8,128)(2,1)S(1)} collective-permute-done((bf16[2,4,256,256]{3,2,1,0:T(8,128)(2,1)S(1)}, bf16[2,4,256,256]{3,2,1,0:T(8,128)(2,1)S(1)}, u32[]{:S(2)}, u32[]{:S(2)}) %collective-permute-start.34) | collective-permute-done | bytes 1048608 | tf_op jit(solution)/shard_map/ppermute | solution.py:28
  858.2 18.4 %collective-permute-done.31 = bf16[2,4,256,256]{3,2,1,0:T(8,128)(2,1)} collective-permute-done((bf16[2,4,256,256]{3,2,1,0:T(8,128)(2,1)S(1)}, bf16[2,4,256,256]{3,2,1,0:T(8,128)(2,1)}, u32[]{:S(2)}, u32[]{:S(2)}) %collective-permute-start.31) | collective-permute-done | bytes 1048608 | tf_op jit(solution)/shard_map/ppermute | solution.py:28
  880.3 68.5 %collective-permute-done.35 = bf16[2,4,256,256]{3,2,1,0:T(8,128)(2,1)} collective-permute-done((bf16[2,4,256,256]{3,2,1,0:T(8,128)(2,1)}, bf16[2,4,256,256]{3,2,1,0:T(8,128)(2,1)}, u32[]{:S(2)}, u32[]{:S(2)}) %collective-permute-start.35) | collective-permute-done | bytes 1048608 | tf_op jit(solution)/shard_map/ppermute | solution.py:28
  980.1 36.0 %collective-permute-done.29 = bf16[768,2048]{1,0:T(8,128)(2,1)} collective-permute-done((bf16[768,2048]{1,0:T(8,128)(2,1)}, bf16[768,2048]{1,0:T(8,128)(2,1)}, u32[]{:S(2)}, u32[]{:S(2)}) %collective-permute-start.29) | collective-permute-done | bytes 3145760 | tf_op jit(solution)/shard_map/ppermute | solution.py:28
  1022.5 61.1 %collective-permute-done.13 = bf16[768,2048]{1,0:T(8,128)(2,1)} collective-permute-done((bf16[768,2048]{1,0:T(8,128)(2,1)}, bf16[768,2048]{1,0:T(8,128)(2,1)}, u32[]{:S(2)}, u32[]{:S(2)}) %collective-permute-start.13) | collective-permute-done | bytes 3145760 | tf_op jit(solution)/shard_map/ppermute | solution.py:28
  1094.0 54.4 %collective-permute-done.25 = bf16[768,2048]{1,0:T(8,128)(2,1)} collective-permute-done((bf16[768,2048]{1,0:T(8,128)(2,1)}, bf16[768,2048]{1,0:T(8,128)(2,1)}, u32[]{:S(2)}, u32[]{:S(2)}) %collective-permute-start.25) | collective-permute-done | bytes 3145760 | tf_op jit(solution)/shard_map/ppermute | solution.py:28
  1165.7 13.1 %reshape.73 = bf16[4,2,8,32,4,2,256]{6,5,4,3,2,1,0:T(2,128)(2,1)} reshape(bf16[4,2,8,256,256]{4,3,2,1,0:T(8,128)(2,1)} %pad_maximum_fusion) | data formatting | bytes 16777216 | tf_op jit(solution)/shard_map/reshape | solution.py:287
  1213.7 10.9 reshape.75
  (221 shorter events, 330.8 us)
Async XLA Ops:
  60.4 154.8 %collective-permute-start.6 = (bf16[768,2048]{1,0:T(8,128)(2,1)S(1)}, bf16[768,2048]{1,0:T(8,128)(2,1)}, u32[]{:S(2)}, u32[]{:S(2)}) collective-permute-start(bf16[768,2048]{1,0:T(8,128)(2,1)S(1)} %get-tuple-element.100.x_ref.up_ref), channel_id=1, source_target_pairs={{0,2},{1,3},{2,0},{3,1},{4,6},{5,7},{6,4},{7,5},{8,10},{9,11},{10,... | collective-permute-start | bytes 9437192 | tf_op jit(solution)/shard_map/ppermute | solution.py:28
  62.5 152.8 %collective-permute-start.8 = (bf16[768,2048]{1,0:T(8,128)(2,1)S(1)}, bf16[768,2048]{1,0:T(8,128)(2,1)S(1)}, u32[]{:S(2)}, u32[]{:S(2)}) collective-permute-start(bf16[768,2048]{1,0:T(8,128)(2,1)S(1)} %get-tuple-element.100.x_ref.up_ref), channel_id=1, source_target_pairs={{0,1},{1,0},{2,3},{3,2},{4,5},{5,4},{6,7},{7,6},{8,9},{9,8},{10,11... | collective-permute-start | bytes 9437192 | tf_op jit(solution)/shard_map/ppermute | solution.py:28
  102.8 179.9 %collective-permute-start = (bf16[768,2048]{1,0:T(8,128)(2,1)S(1)}, bf16[768,2048]{1,0:T(8,128)(2,1)}, u32[]{:S(2)}, u32[]{:S(2)}) collective-permute-start(bf16[768,2048]{1,0:T(8,128)(2,1)S(1)} %get-tuple-element.102.x_ref), channel_id=1, source_target_pairs={{0,2},{1,3},{2,0},{3,1},{4,6},{5,7},{6,4},{7,5},{8,10},{9,11},{10,... | collective-permute-start | bytes 9437192 | tf_op jit(solution)/shard_map/ppermute | solution.py:28
  104.9 177.8 %collective-permute-start.3 = (bf16[768,2048]{1,0:T(8,128)(2,1)S(1)}, bf16[768,2048]{1,0:T(8,128)(2,1)S(1)}, u32[]{:S(2)}, u32[]{:S(2)}) collective-permute-start(bf16[768,2048]{1,0:T(8,128)(2,1)S(1)} %get-tuple-element.102.x_ref), channel_id=1, source_target_pairs={{0,1},{1,0},{2,3},{3,2},{4,5},{5,4},{6,7},{7,6},{8,9},{9,8},{10,11... | collective-permute-start | bytes 9437192 | tf_op jit(solution)/shard_map/ppermute | solution.py:28
  147.4 202.7 %collective-permute-start.18 = (bf16[768,2048]{1,0:T(8,128)(2,1)S(1)}, bf16[768,2048]{1,0:T(8,128)(2,1)}, u32[]{:S(2)}, u32[]{:S(2)}) collective-permute-start(bf16[768,2048]{1,0:T(8,128)(2,1)S(1)} %get-tuple-element.101.x_ref.up_ref), channel_id=1, source_target_pairs={{0,2},{1,3},{2,0},{3,1},{4,6},{5,7},{6,4},{7,5},{8,10},{9,11},{10,... | collective-permute-start | bytes 9437192 | tf_op jit(solution)/shard_map/ppermute | solution.py:28
  215.3 158.0 %collective-permute-start.20 = (bf16[768,2048]{1,0:T(8,128)(2,1)S(1)}, bf16[768,2048]{1,0:T(8,128)(2,1)}, u32[]{:S(2)}, u32[]{:S(2)}) collective-permute-start(bf16[768,2048]{1,0:T(8,128)(2,1)S(1)} %get-tuple-element.101.x_ref.up_ref), channel_id=1, source_target_pairs={{0,1},{1,0},{2,3},{3,2},{4,5},{5,4},{6,7},{7,6},{8,9},{9,8},{10,11... | collective-permute-start | bytes 9437192 | tf_op jit(solution)/shard_map/ppermute | solution.py:28
  216.9 199.7 %collective-permute-start.15 = (bf16[768,2048]{1,0:T(8,128)(2,1)}, bf16[768,2048]{1,0:T(8,128)(2,1)}, u32[]{:S(2)}, u32[]{:S(2)}) collective-permute-start(bf16[768,2048]{1,0:T(8,128)(2,1)} %get-tuple-element.103.x_ref), channel_id=1, source_target_pairs={{0,2},{1,3},{2,0},{3,1},{4,6},{5,7},{6,4},{7,5},{8,10},{9,11},{10,... | collective-permute-start | bytes 9437192 | tf_op jit(solution)/shard_map/ppermute | solution.py:28
  282.7 160.9 %collective-permute-start.17 = (bf16[768,2048]{1,0:T(8,128)(2,1)}, bf16[768,2048]{1,0:T(8,128)(2,1)}, u32[]{:S(2)}, u32[]{:S(2)}) collective-permute-start(bf16[768,2048]{1,0:T(8,128)(2,1)} %get-tuple-element.103.x_ref), channel_id=1, source_target_pairs={{0,1},{1,0},{2,3},{3,2},{4,5},{5,4},{6,7},{7,6},{8,9},{9,8},{10,11... | collective-permute-start | bytes 9437192 | tf_op jit(solution)/shard_map/ppermute | solution.py:28
  284.4 164.3 %collective-permute-start.7 = (bf16[768,2048]{1,0:T(8,128)(2,1)}, bf16[768,2048]{1,0:T(8,128)(2,1)}, u32[]{:S(2)}, u32[]{:S(2)}) collective-permute-start(bf16[768,2048]{1,0:T(8,128)(2,1)} %collective-permute-done.6.x_ref.up_ref), channel_id=1, source_target_pairs={{0,1},{1,0},{2,3},{3,2},{4,5},{5,4},{6,7},{7,6},{8,9},{9,8},{10,11... | collective-permute-start | bytes 9437192 | tf_op jit(solution)/shard_map/ppermute | solution.py:28
  373.2 151.3 %collective-permute-start.19 = (bf16[768,2048]{1,0:T(8,128)(2,1)}, bf16[768,2048]{1,0:T(8,128)(2,1)}, u32[]{:S(2)}, u32[]{:S(2)}) collective-permute-start(bf16[768,2048]{1,0:T(8,128)(2,1)} %collective-permute-done.18.x_ref.up_ref), channel_id=1, source_target_pairs={{0,1},{1,0},{2,3},{3,2},{4,5},{5,4},{6,7},{7,6},{8,9},{9,8},{10,11... | collective-permute-start | bytes 9437192 | tf_op jit(solution)/shard_map/ppermute | solution.py:28
  512.8 128.9 %collective-permute-start.10 = (bf16[768,2048]{1,0:T(8,128)(2,1)}, bf16[768,2048]{1,0:T(8,128)(2,1)}, u32[]{:S(2)}, u32[]{:S(2)}) collective-permute-start(bf16[768,2048]{1,0:T(8,128)(2,1)} %get-tuple-element.49), channel_id=1, source_target_pairs={{0,1},{1,0},{2,3},{3,2},{4,5},{5,4},{6,7},{7,6},{8,9},{9,8},{10,11... | collective-permute-start | bytes 9437192 | tf_op jit(solution)/shard_map/ppermute | solution.py:28
  524.1 118.3 %collective-permute-start.12 = (bf16[768,2048]{1,0:T(8,128)(2,1)}, bf16[768,2048]{1,0:T(8,128)(2,1)}, u32[]{:S(2)}, u32[]{:S(2)}) collective-permute-start(bf16[768,2048]{1,0:T(8,128)(2,1)} %get-tuple-element.52), channel_id=1, source_target_pairs={{0,1},{1,0},{2,3},{3,2},{4,5},{5,4},{6,7},{7,6},{8,9},{9,8},{10,11... | collective-permute-start | bytes 9437192 | tf_op jit(solution)/shard_map/ppermute | solution.py:28
  648.9 305.5 %collective-permute-start.40 = (bf16[32,256,256]{2,1,0:T(8,128)(2,1)}, bf16[32,256,256]{2,1,0:T(8,128)(2,1)}, u32[]{:S(2)}, u32[]{:S(2)}) collective-permute-start(bf16[32,256,256]{2,1,0:T(8,128)(2,1)} %convert_element_type.159), channel_id=1, source_target_pairs={{0,16},{16,0},{1,17},{17,1},{2,18},{18,2},{3,19},{19,3},{4,20},{20... | collective-permute-start | bytes 12582920 | tf_op jit(solution)/shard_map/ppermute | solution.py:28
  655.0 299.7 %collective-permute-start.39 = (bf16[32,256,256]{2,1,0:T(8,128)(2,1)}, bf16[32,256,256]{2,1,0:T(8,128)(2,1)}, u32[]{:S(2)}, u32[]{:S(2)}) collective-permute-start(bf16[32,256,256]{2,1,0:T(8,128)(2,1)} %convert_element_type.156), channel_id=1, source_target_pairs={{0,16},{16,0},{1,17},{17,1},{2,18},{18,2},{3,19},{19,3},{4,20},{20... | collective-permute-start | bytes 12582920 | tf_op jit(solution)/shard_map/ppermute | solution.py:28
  683.2 171.7 %collective-permute-start.34 = (bf16[2,4,256,256]{3,2,1,0:T(8,128)(2,1)S(1)}, bf16[2,4,256,256]{3,2,1,0:T(8,128)(2,1)S(1)}, u32[]{:S(2)}, u32[]{:S(2)}) collective-permute-start(bf16[2,4,256,256]{3,2,1,0:T(8,128)(2,1)S(1)} %fusion.7), channel_id=1, source_target_pairs={{0,16},{16,0},{1,17},{17,1},{2,18},{18,2},{3,19},{19,3},{4,20},{20... | collective-permute-start | bytes 3145736 | tf_op jit(solution)/shard_map/ppermute | solution.py:28
  685.1 172.9 %collective-permute-start.37 = (bf16[2,4,256,256]{3,2,1,0:T(8,128)(2,1)S(1)}, bf16[2,4,256,256]{3,2,1,0:T(8,128)(2,1)}, u32[]{:S(2)}, u32[]{:S(2)}) collective-permute-start(bf16[2,4,256,256]{3,2,1,0:T(8,128)(2,1)S(1)} %fusion.5), channel_id=1, source_target_pairs={{0,3},{1,2},{2,1},{3,0},{4,7},{5,6},{6,5},{7,4},{8,11},{9,10},{10,... | collective-permute-start | bytes 3145736 | tf_op jit(solution)/shard_map/ppermute | solution.py:28
  712.0 164.6 %collective-permute-start.31 = (bf16[2,4,256,256]{3,2,1,0:T(8,128)(2,1)S(1)}, bf16[2,4,256,256]{3,2,1,0:T(8,128)(2,1)}, u32[]{:S(2)}, u32[]{:S(2)}) collective-permute-start(bf16[2,4,256,256]{3,2,1,0:T(8,128)(2,1)S(1)} %fusion.17), channel_id=1, source_target_pairs={{0,16},{16,0},{1,17},{17,1},{2,18},{18,2},{3,19},{19,3},{4,20},{20... | collective-permute-start | bytes 3145736 | tf_op jit(solution)/shard_map/ppermute | solution.py:28
  876.6 139.5 %collective-permute-start.29 = (bf16[768,2048]{1,0:T(8,128)(2,1)}, bf16[768,2048]{1,0:T(8,128)(2,1)}, u32[]{:S(2)}, u32[]{:S(2)}) collective-permute-start(bf16[768,2048]{1,0:T(8,128)(2,1)} %get-tuple-element.75), channel_id=1, source_target_pairs={{0,2},{1,3},{2,0},{3,1},{4,6},{5,7},{6,4},{7,5},{8,10},{9,11},{10,... | collective-permute-start | bytes 9437192 | tf_op jit(solution)/shard_map/ppermute | solution.py:28
  948.7 134.8 %collective-permute-start.13 = (bf16[768,2048]{1,0:T(8,128)(2,1)}, bf16[768,2048]{1,0:T(8,128)(2,1)}, u32[]{:S(2)}, u32[]{:S(2)}) collective-permute-start(bf16[768,2048]{1,0:T(8,128)(2,1)} %get-tuple-element.53), channel_id=1, source_target_pairs={{0,2},{1,3},{2,0},{3,1},{4,6},{5,7},{6,4},{7,5},{8,10},{9,11},{10,... | collective-permute-start | bytes 9437192 | tf_op jit(solution)/shard_map/ppermute | solution.py:28
  954.5 194.0 %collective-permute-start.25 = (bf16[768,2048]{1,0:T(8,128)(2,1)}, bf16[768,2048]{1,0:T(8,128)(2,1)}, u32[]{:S(2)}, u32[]{:S(2)}) collective-permute-start(bf16[768,2048]{1,0:T(8,128)(2,1)} %get-tuple-element.71), channel_id=1, source_target_pairs={{0,2},{1,3},{2,0},{3,1},{4,6},{5,7},{6,4},{7,5},{8,10},{9,11},{10,... | collective-permute-start | bytes 9437192 | tf_op jit(solution)/shard_map/ppermute | solution.py:28
  954.7 203.9 %collective-permute-start.38 = (bf16[4,2,4,256,256]{4,3,2,1,0:T(8,128)(2,1)}, bf16[4,2,4,256,256]{4,3,2,1,0:T(8,128)(2,1)S(1)}, u32[]{:S(2)}, u32[]{:S(2)}) collective-permute-start(bf16[4,2,4,256,256]{4,3,2,1,0:T(8,128)(2,1)} %pad_maximum_fusion.1), channel_id=1, source_target_pairs={{0,16},{16,0},{1,17},{17,1},{2,18},{18,2},{3,19},{19,3},{4,20},{20... | collective-permute-start | bytes 12582920 | tf_op jit(solution)/shard_map/ppermute | solution.py:28
  978.8 245.7 %collective-permute-start.28 = (bf16[768,2048]{1,0:T(8,128)(2,1)}, bf16[768,2048]{1,0:T(8,128)(2,1)}, u32[]{:S(2)}, u32[]{:S(2)}) collective-permute-start(bf16[768,2048]{1,0:T(8,128)(2,1)} %add_convert_fusion.1), channel_id=1, source_target_pairs={{4,0},{8,4},{12,8},{5,1},{9,5},{13,9},{6,2},{10,6},{14,10},{7,3},{... | collective-permute-start | bytes 9437192 | tf_op jit(solution)/shard_map/ppermute | solution.py:34
  1021.2 203.3 %collective-permute-start.30 = (bf16[768,2048]{1,0:T(8,128)(2,1)}, bf16[768,2048]{1,0:T(8,128)(2,1)}, u32[]{:S(2)}, u32[]{:S(2)}) collective-permute-start(bf16[768,2048]{1,0:T(8,128)(2,1)} %add_convert_fusion), channel_id=1, source_target_pairs={{4,0},{8,4},{12,8},{5,1},{9,5},{13,9},{6,2},{10,6},{14,10},{7,3},{... | collective-permute-start | bytes 9437192 | tf_op jit(solution)/shard_map/ppermute | solution.py:34
  1088.7 142.5 %collective-permute-start.14 = (bf16[768,2048]{1,0:T(8,128)(2,1)}, bf16[768,2048]{1,0:T(8,128)(2,1)}, u32[]{:S(2)}, u32[]{:S(2)}) collective-permute-start(bf16[768,2048]{1,0:T(8,128)(2,1)} %add_convert_fusion.3), channel_id=1, source_target_pairs={{0,4},{4,8},{8,12},{1,5},{5,9},{9,13},{2,6},{6,10},{10,14},{3,7},{... | collective-permute-start | bytes 9437192 | tf_op jit(solution)/shard_map/ppermute | solution.py:34
  (62 other events, 2502.2 us)
